TPU v7x, 512 devices: a whole 4x8x8 slice. The times are simulated.
512 devices in a mesh: bx: 32 (over z_hi, y, core), by: 16 (over x, z_lo).
Axes of the slice: x: 4, y: 8, z: 8 (z_hi: 2, z_lo: 4; z = z_hi * 4 + z_lo), core: 2. Of those that a mesh axis runs over, the one named last changes fastest.
Arguments:
- interface_velocity: float32 [3, 2048, 2048], P(None, 'bx', 'by'), may hold values from -6 to 6
- history: float32 [6, 2, 3, 64, 32, 16, 128], P(None, None, None, 'by', 'bx'), may hold values from -6 to 6
- kernel: float32 [7, 64, 32, 16, 128], P(None, 'by', 'bx'), may hold values from -6 to 6
- velocity: float32 [3, 4, 2048, 2048], P(None, None, 'bx', 'by'), may hold values from -6 to 6
- stress: float32 [6, 4, 2048, 2048], P(None, None, 'bx', 'by'), may hold values from -6 to 6
- cohesion: float32 [4, 2048, 2048], P(None, 'bx', 'by'), may hold values from 0.5 to 4
Outputs:
- velocity_new: float32 [3, 4, 2048, 2048], P(None, None, 'bx', 'by')
- stress_new: float32 [6, 4, 2048, 2048], P(None, None, 'bx', 'by')
All inputs are finite; a program needn't handle non-finite values.
Results may differ from a plain program's by a relative error of at most 0.00005.
Values sent between devices are 32-bit elements; how exact they have to be, the bound alone decides.
No kernel may reach another device: no remote copies, remote signals or barrier semaphores. Data moves between devices by JAX's collectives and lax.ppermute only.
A program may use at most 64 MiB of HBM per device.

v0:
```python
from functools import partial
import math
import jax
import jax.numpy as jnp
from jax import lax
from jax.sharding import PartitionSpec as P

COURANT = 0.3
FRICTION = 0.6
HIGHEST = lax.Precision.HIGHEST


def extended(block, sides, width):
    for axis, dim in sides:
        count = lax.axis_size(axis)
        forward = [(i, i + 1) for i in range(count - 1)]
        forward.append((count - 1, 0))
        backward = [(target, source) for source, target in forward]
        low = lax.ppermute(
            lax.slice_in_dim(block, block.shape[dim] - width, None, axis=dim), axis, forward
        )
        high = lax.ppermute(lax.slice_in_dim(block, 0, width, axis=dim), axis, backward)
        block = jnp.concatenate([low, block, high], axis=dim)
    return block


def counting(count):
    return jnp.arange(count, dtype=jnp.int32)


def phase_table(row_index, col_index, length, sign):
    product = row_index[:, None] * col_index[None, :] % length
    angle = 2.0 * math.pi / length * product.astype(jnp.float32)
    return (jnp.cos(angle), sign * jnp.sin(angle))


def conjugate(table):
    return (table[0], -table[1])


def complex_apply(pattern, real_part, imag_part, table):
    contract = partial(jnp.einsum, pattern, precision=HIGHEST)
    return (
        contract(real_part, table[0]) - contract(imag_part, table[1]),
        contract(real_part, table[1]) + contract(imag_part, table[0]),
    )


def twist(real_part, imag_part, table_real, table_imag):
    return (
        real_part * table_real - imag_part * table_imag,
        real_part * table_imag + imag_part * table_real,
    )


def dip_blocks(block):
    return lax.all_to_all(block, "by", split_axis=2, concat_axis=2, tiled=True)


def strike_modes(block):
    return lax.all_to_all(block, "bx", split_axis=4, concat_axis=4, tiled=True)


def widen(fields):
    return extended(fields, (("bx", 2), ("by", 3)), 1)


def strike_diff(padded):
    return 0.5 * (padded[..., 2:, 1:-1] - padded[..., :-2, 1:-1])


def dip_diff(padded):
    return 0.5 * (padded[..., 1:-1, 2:] - padded[..., 1:-1, :-2])


def depth_diff(layered, ghost_layer):
    above_layer = jnp.concatenate([layered[1:], jnp.zeros_like(layered[:1])], axis=0)
    below_layer = jnp.concatenate([ghost_layer[None], layered[:-1]], axis=0)
    return 0.5 * (above_layer - below_layer)


def yield_limit(trial_stress, cohesion):
    pressure = (trial_stress[0] + trial_stress[1] + trial_stress[2]) / 3.0
    normal_dev = trial_stress[:3] - pressure[None]
    second = 0.5 * jnp.sum(normal_dev * normal_dev, axis=0) + jnp.sum(
        trial_stress[3:] * trial_stress[3:], axis=0
    )
    shear_stress = jnp.sqrt(second)
    yield_stress = cohesion + FRICTION * jnp.maximum(-pressure, 0.0)
    factor = yield_stress / jnp.maximum(shear_stress, yield_stress)
    return jnp.concatenate(
        [pressure[None] + factor[None] * normal_dev, factor[None] * trial_stress[3:]], axis=0
    )


def advance_bulk(velocity, stress, traction, interface_velocity, cohesion):
    padded_stress = widen(stress)
    forcing = jnp.stack(
        [
            strike_diff(padded_stress[0])
            + dip_diff(padded_stress[3])
            + depth_diff(stress[4], traction[0]),
            strike_diff(padded_stress[3])
            + dip_diff(padded_stress[1])
            + depth_diff(stress[5], traction[1]),
            strike_diff(padded_stress[4])
            + dip_diff(padded_stress[5])
            + depth_diff(stress[2], traction[2]),
        ]
    )
    velocity_new = velocity + COURANT * forcing
    padded_velocity = widen(velocity_new)
    strike_grad = strike_diff(padded_velocity)
    dip_grad = dip_diff(padded_velocity)
    depth_grad = jnp.stack(
        [
            depth_diff(velocity_new[component], interface_velocity[component])
            for component in range(3)
        ]
    )
    dilation = strike_grad[0] + dip_grad[1] + depth_grad[2]
    rates = jnp.stack(
        [
            dilation + 2.0 * strike_grad[0],
            dilation + 2.0 * dip_grad[1],
            dilation + 2.0 * depth_grad[2],
            dip_grad[0] + strike_grad[1],
            depth_grad[0] + strike_grad[2],
            depth_grad[1] + dip_grad[2],
        ]
    )
    trial_stress = stress + COURANT * rates
    return (velocity_new, yield_limit(trial_stress, cohesion))


def local(interface_velocity, history, kernel, velocity, stress, cohesion):
    strike_count = lax.axis_size("bx")
    dip_count = lax.axis_size("by")
    strike_index = lax.axis_index("bx")
    strike_cells = interface_velocity.shape[1]
    dip_cells = interface_velocity.shape[2]
    row_block = dip_cells // strike_count
    mode_block = strike_cells // dip_count
    strike_length = strike_cells * strike_count
    dip_length = dip_cells * dip_count
    scale = 1.0 / math.sqrt(strike_length * dip_length)
    strike_table = phase_table(counting(strike_count), counting(strike_count), strike_count, -1.0)
    strike_twist = phase_table(counting(strike_cells), counting(strike_count), strike_length, -1.0)
    cell_table = phase_table(counting(strike_cells), counting(strike_cells), strike_cells, -1.0)
    dip_table = phase_table(counting(dip_count), counting(dip_count), dip_count, -1.0)
    column_table = phase_table(counting(dip_cells), counting(dip_cells), dip_cells, -1.0)
    gathered = lax.all_gather(interface_velocity, "bx", axis=1, tiled=True)
    own_columns = lax.dynamic_slice_in_dim(gathered, strike_index * row_block, row_block, 2)
    grouped = own_columns.reshape(3, strike_count, strike_cells, row_block)
    first_pattern = "cpqr,pk->cqkr"
    real_part = jnp.einsum(first_pattern, grouped, strike_table[0], precision=HIGHEST)
    imag_part = jnp.einsum(first_pattern, grouped, strike_table[1], precision=HIGHEST)
    real_part, imag_part = twist(
        real_part, imag_part, strike_twist[0][None, :, :, None], strike_twist[1][None, :, :, None]
    )
    real_part, imag_part = complex_apply("cqkr,qm->cmkr", real_part, imag_part, cell_table)
    stacked = jnp.stack([real_part, imag_part])
    dip_offsets = row_block * strike_index + counting(row_block)
    dip_twist = phase_table(counting(dip_count), dip_offsets, dip_length, -1.0)
    arrived = dip_blocks(stacked.reshape(2, 3, strike_cells, dip_cells))
    arrived = arrived.reshape(2, 3, dip_count, mode_block, strike_count, row_block)
    real_part, imag_part = complex_apply("cjukr,jl->clukr", arrived[0], arrived[1], dip_table)
    real_part, imag_part = twist(
        real_part,
        imag_part,
        dip_twist[0][None, :, None, None, :],
        dip_twist[1][None, :, None, None, :],
    )
    arrived = strike_modes(
        jnp.stack([real_part, imag_part]).reshape(2, 3, dip_count, mode_block, dip_cells)
    )
    real_part, imag_part = (arrived[0], arrived[1])
    real_part, imag_part = complex_apply("clus,sm->culm", real_part, imag_part, column_table)
    spectrum = scale * jnp.stack([real_part, imag_part])[:, :, :, None]
    past_terms = jnp.einsum("hupks,hzcupks->zcupks", kernel[1:], history, precision=HIGHEST)
    response = kernel[0][None, None] * spectrum + past_terms
    real_part, imag_part = complex_apply(
        "cuks,sm->ckum", response[0, :, :, 0], response[1, :, :, 0], conjugate(column_table)
    )
    dip_offsets = row_block * strike_index + counting(row_block)
    back_twist = conjugate(phase_table(counting(dip_count), dip_offsets, dip_length, -1.0))
    arrived = strike_modes(jnp.stack([real_part, imag_part]))
    arrived = arrived.reshape(2, 3, dip_count, mode_block, strike_count, row_block)
    real_part, imag_part = twist(
        arrived[0],
        arrived[1],
        back_twist[0][None, :, None, None, :],
        back_twist[1][None, :, None, None, :],
    )
    real_part, imag_part = complex_apply(
        "clukr,lj->cjukr", real_part, imag_part, conjugate(dip_table)
    )
    arrived = dip_blocks(jnp.stack([real_part, imag_part]).reshape(2, 3, strike_cells, dip_cells))
    arrived = arrived.reshape(2, 3, strike_cells, strike_count, row_block)
    real_part, imag_part = complex_apply(
        "cmkr,mq->cqkr", arrived[0], arrived[1], conjugate(cell_table)
    )
    back_strike = conjugate(strike_twist)
    real_part, imag_part = twist(
        real_part, imag_part, back_strike[0][None, :, :, None], back_strike[1][None, :, :, None]
    )
    inverse_table = conjugate(strike_table)
    spatial = jnp.einsum(
        "cqkr,kp->cpqr", real_part, inverse_table[0], precision=HIGHEST
    ) - jnp.einsum("cqkr,kp->cpqr", imag_part, inverse_table[1], precision=HIGHEST)
    gathered = lax.all_gather(
        spatial.reshape(3, strike_length, row_block), "bx", axis=2, tiled=True
    )
    traction = scale * lax.dynamic_slice_in_dim(
        gathered, strike_index * strike_cells, strike_cells, 1
    )
    velocity_new, stress_new = advance_bulk(
        velocity, stress, traction, interface_velocity, cohesion
    )
    return (velocity_new, stress_new)


def solution(mesh):
    return jax.shard_map(
        local,
        mesh=mesh,
        in_specs=(
            P(None, "bx", "by"),
            P(None, None, None, "by", "bx", None, None),
            P(None, "by", "bx", None, None),
            P(None, None, "bx", "by"),
            P(None, None, "bx", "by"),
            P(None, "bx", "by"),
        ),
        out_specs=(P(None, None, "bx", "by"), P(None, None, "bx", "by")),
        check_vma=False,
    )
```

profile of v0, /device:TPU:6, one launch (start us, length us, event | category | flops | bytes accessed | tf_op | source)
XLA Modules:
  0.0 402.0 jit_solution(16210227547957793094)
XLA Ops:
  8.0 108.7 %all-gather.3.cloned.1.call-done = f32[3,2048,128]{2,1,0:T(8,128)} async-done(((f32[3,64,128]{2,1,0:T(8,128)}), f32[3,2048,128]{2,1,0:T(8,128)}) %all-gather.3.cloned.1.call-update) | async-done | bytes 3145744 | tf_op jit(solution)/shard_map/all_gather | solution.py:152
  116.7 2.8 constant_dynamic-slice_fusion
  124.5 5.9 %all-to-all-start = ((f32[2,3,64,128]{3,0,1,2:T(2,128)}), f32[2,3,64,128]{3,0,1,2:T(2,128)S(1)}, u32[]{:S(2)}, u32[]{:S(2)}) async-start(f32[2,3,64,128]{3,0,1,2:T(2,128)} %copy.159), calls=%async_computation | async-start | bytes 393216 | tf_op jit(solution)/shard_map/all_to_all | solution.py:57
  131.8 6.1 %all-to-all-done = f32[2,3,64,128]{3,0,1,2:T(2,128)S(1)} async-done(((f32[2,3,64,128]{3,0,1,2:T(2,128)}), f32[2,3,64,128]{3,0,1,2:T(2,128)S(1)}, u32[]{:S(2)}, u32[]{:S(2)}) %all-to-all-start) | async-done | bytes 196640 | tf_op jit(solution)/shard_map/all_to_all | solution.py:57
  139.0 3.4 reshape.256
  146.6 4.2 %reshape.257 = f32[3,16,4,32,4]{4,3,0,2,1:T(8,128)S(1)} reshape(f32[3,64,128]{2,0,1:T(4,128)} %get-tuple-element.10) | data formatting | bytes 196608 | tf_op jit(solution)/shard_map/squeeze | solution.py:167
  157.4 1.9 reshape.260
  159.3 6.0 %all-to-all-start.1 = ((f32[32,1,1536]{2,1,0:T(1,128)}), f32[32,1,1536]{2,1,0:T(1,128)S(1)}, u32[]{:S(2)}, u32[]{:S(2)}) async-start(f32[32,1,1536]{2,1,0:T(1,128)} %reshape.260), calls=%async_computation.1 | async-start | bytes 393216 | tf_op jit(solution)/shard_map/all_to_all | solution.py:61
  166.8 14.2 %all-to-all-done.1 = f32[32,1,1536]{2,1,0:T(1,128)S(1)} async-done(((f32[32,1,1536]{2,1,0:T(1,128)}), f32[32,1,1536]{2,1,0:T(1,128)S(1)}, u32[]{:S(2)}, u32[]{:S(2)}) %all-to-all-start.1) | async-done | bytes 196640 | tf_op jit(solution)/shard_map/all_to_all | solution.py:61
  190.7 18.9 %all_to_all.20 = f32[32,1,1536]{2,1,0:T(1,128)S(1)} all-to-all(f32[32,1,1536]{2,1,0:T(1,128)S(1)} %reshape.262), channel_id=1, replica_groups=mesh['bx'=32,'by'=16] {'bx'}, dimensions={0} | all-to-all | bytes 393216 | tf_op jit(solution)/shard_map/all_to_all | solution.py:61
  216.6 2.2 copy.176
  218.8 3.2 stack.88
  224.9 2.6 stack.89
  228.4 5.8 %all-to-all-start.3 = ((f32[2,3,64,128]{3,0,1,2:T(2,128)}), f32[2,3,64,128]{3,0,1,2:T(2,128)S(1)}, u32[]{:S(2)}, u32[]{:S(2)}) async-start(f32[2,3,64,128]{3,0,1,2:T(2,128)} %copy.180), calls=%async_computation.3 | async-start | bytes 393216 | tf_op jit(solution)/shard_map/all_to_all | solution.py:57
  234.5 6.3 %all-to-all-done.3 = f32[2,3,64,128]{3,0,1,2:T(2,128)S(1)} async-done(((f32[2,3,64,128]{3,0,1,2:T(2,128)}), f32[2,3,64,128]{3,0,1,2:T(2,128)S(1)}, u32[]{:S(2)}, u32[]{:S(2)}) %all-to-all-start.3) | async-done | bytes 196640 | tf_op jit(solution)/shard_map/all_to_all | solution.py:57
  244.8 1.9 collective-permute-start
  246.8 9.7 %collective-permute-start.1 = (f32[6,4,1,128]{3,1,2,0:T(4,128)S(1)}, f32[6,4,1,128]{3,1,2,0:T(4,128)S(1)}, u32[]{:S(2)}, u32[]{:S(2)}) collective-permute-start(f32[6,4,1,128]{3,1,2,0:T(4,128)S(1)} %bitcast.319), channel_id=1, source_target_pairs={{16,0},{32,16},{48,32},{64,48},{80,64},{96,80},{112,96},{128,112},... | collective-permute-start | bytes 36872 | tf_op jit(solution)/shard_map/ppermute | solution.py:22
  260.3 2.7 collective-permute-start.2
  263.0 5.9 %collective-permute-start.3 = (f32[6,4,66,1]{2,1,3,0:T(4,128)S(1)}, f32[6,4,66,1]{2,1,3,0:T(4,128)S(1)}, u32[]{:S(2)}, u32[]{:S(2)}) collective-permute-start(f32[6,4,66,1]{2,1,3,0:T(4,128)S(1)} %get-tuple-element.20), channel_id=1, source_target_pairs={{1,0},{2,1},{3,2},{4,3},{5,4},{6,5},{7,6},{8,7},{9,8},{10,9},{11,1... | collective-permute-start | bytes 19016 | tf_op jit(solution)/shard_map/ppermute | solution.py:22
  270.1 2.1 copy.193
  272.3 2.5 maximum_bitcast_fusion.2
  274.7 1.8 maximum_bitcast_fusion.3
  276.6 68.3 %all-gather.5.cloned.1.call-done = f32[3,2048,128]{1,0,2:T(4,128)} async-done(((f32[3,2048,4]{1,0,2:T(4,128)}), f32[3,2048,128]{1,0,2:T(4,128)}) %all-gather.5.cloned.1.call-update) | async-done | bytes 3145744 | tf_op jit(solution)/shard_map/all_gather | solution.py:211
  346.1 1.9 fusion.27
  352.4 1.9 collective-permute-start.4
  355.2 2.4 collective-permute-start.5
  359.7 6.7 %collective-permute-done.5 = f32[3,4,1,128]{3,1,2,0:T(4,128)} collective-permute-done((f32[3,4,1,128]{3,1,2,0:T(4,128)}, f32[3,4,1,128]{3,1,2,0:T(4,128)}, u32[]{:S(2)}, u32[]{:S(2)}) %collective-permute-start.5) | collective-permute-done | bytes 6176 | tf_op jit(solution)/shard_map/ppermute | solution.py:19
  366.4 1.9 copy.197
  369.7 5.9 %collective-permute-start.6 = (f32[3,4,66,1]{2,1,3,0:T(4,128)}, f32[3,4,66,1]{2,1,3,0:T(4,128)S(1)}, u32[]{:S(2)}, u32[]{:S(2)}) collective-permute-start(f32[3,4,66,1]{2,1,3,0:T(4,128)} %get-tuple-element.23), channel_id=1, source_target_pairs={{1,0},{2,1},{3,2},{4,3},{5,4},{6,5},{7,6},{8,7},{9,8},{10,9},{11,1... | collective-permute-start | bytes 9512 | tf_op jit(solution)/shard_map/ppermute | solution.py:22
  375.6 2.2 collective-permute-start.7
  380.0 4.0 %collective-permute-done.7 = f32[3,4,66,1]{2,1,3,0:T(4,128)S(1)} collective-permute-done((f32[3,4,66,1]{2,1,3,0:T(4,128)}, f32[3,4,66,1]{2,1,3,0:T(4,128)S(1)}, u32[]{:S(2)}, u32[]{:S(2)}) %collective-permute-start.7) | collective-permute-done | bytes 3200 | tf_op jit(solution)/shard_map/ppermute | solution.py:19
  384.1 4.8 %fusion.11 = (f32[3,4,64,128]{2,1,3,0:T(4,128)S(1)}, f32[3,4,64,128]{2,1,3,0:T(4,128)S(1)}) fusion(f32[3,4,66,1]{2,1,3,0:T(4,128)S(1)} %collective-permute-done.7, f32[3,4,1,128]{2,1,3,0:T(4,128)S(1)} %copy.195, f32[3,4,64,128]{2,1,3,0:T(4,128)S(1)} %fusion.14, f32[3,4,1,128]{2,1,3,0:T(4,128)} %copy.197, f32[3,4,66,1]{2,1,3,0:T(4,128)S(1)} %collective-permute-done.6), kind=kLoop, calls=%fused_computation.32 | loop fusion | flops 1179648 | bytes 1198272 | tf_op jit(solution)/shard_map/mul | solution.py:73
  (170 shorter events, 67.8 us)
Async XLA Ops:
  7.2 109.5 %all-gather.3.cloned.1.call-start = ((), (), s32[]{:S(2)}) async-start(), calls=%async_computation.4 | async-start | bytes 3244032 | tf_op jit(solution)/shard_map/all_gather | solution.py:152
  123.1 8.1 %copy-start.20 = (f32[7,4,1,16,128]{4,3,2,1,0:T(8,128)S(1)}, f32[7,4,1,16,128]{4,3,2,1,0:T(8,128)}, u32[]{:S(2)}) copy-start(f32[7,4,1,16,128]{4,3,2,1,0:T(8,128)} %param.8) | copy-start | bytes 688132
  124.5 13.4 %all-to-all-start = ((f32[2,3,64,128]{3,0,1,2:T(2,128)}), f32[2,3,64,128]{3,0,1,2:T(2,128)S(1)}, u32[]{:S(2)}, u32[]{:S(2)}) async-start(f32[2,3,64,128]{3,0,1,2:T(2,128)} %copy.159), calls=%async_computation | async-start | bytes 393216 | tf_op jit(solution)/shard_map/all_to_all | solution.py:57
  157.4 7.9 %copy-start.5 = (f32[6,2,3,4,1,16,128]{6,5,4,3,2,1,0:T(8,128)S(1)}, f32[6,2,3,4,1,16,128]{6,5,4,3,2,1,0:T(8,128)}, u32[]{:S(2)}) copy-start(f32[6,2,3,4,1,16,128]{6,5,4,3,2,1,0:T(8,128)} %param.7) | copy-start | bytes 3538948
  157.4 7.9 %copy-start.16 = (f32[4,16,128,6]{2,1,0,3:T(8,128)S(1)}, f32[4,16,128,6]{2,1,0,3:T(8,128)}, u32[]{:S(2)}) copy-start(f32[4,16,128,6]{2,1,0,3:T(8,128)} %slice_bitcast_fusion.14) | copy-start | bytes 589828
  159.3 21.7 %all-to-all-start.1 = ((f32[32,1,1536]{2,1,0:T(1,128)}), f32[32,1,1536]{2,1,0:T(1,128)S(1)}, u32[]{:S(2)}, u32[]{:S(2)}) async-start(f32[32,1,1536]{2,1,0:T(1,128)} %reshape.260), calls=%async_computation.1 | async-start | bytes 393216 | tf_op jit(solution)/shard_map/all_to_all | solution.py:61
  184.0 2.6 copy-start.22
  224.9 2.6 copy-start.17
  228.4 12.4 %all-to-all-start.3 = ((f32[2,3,64,128]{3,0,1,2:T(2,128)}), f32[2,3,64,128]{3,0,1,2:T(2,128)S(1)}, u32[]{:S(2)}, u32[]{:S(2)}) async-start(f32[2,3,64,128]{3,0,1,2:T(2,128)} %copy.180), calls=%async_computation.3 | async-start | bytes 393216 | tf_op jit(solution)/shard_map/all_to_all | solution.py:57
  234.2 110.7 %all-gather.5.cloned.1.call-start = ((), (), s32[]{:S(2)}) async-start(), calls=%async_computation.5 | async-start | bytes 4325376 | tf_op jit(solution)/shard_map/all_gather | solution.py:211
  242.2 2.6 copy-start.15
  244.8 12.3 %collective-permute-start = (f32[6,4,1,128]{3,1,2,0:T(4,128)S(1)}, f32[6,4,1,128]{3,1,2,0:T(4,128)S(1)}, u32[]{:S(2)}, u32[]{:S(2)}) collective-permute-start(f32[6,4,1,128]{3,1,2,0:T(4,128)S(1)} %bitcast.320), channel_id=1, source_target_pairs={{0,16},{16,32},{32,48},{48,64},{64,80},{80,96},{96,112},{112,128},... | collective-permute-start | bytes 36872 | tf_op jit(solution)/shard_map/ppermute | solution.py:19
  246.8 11.2 %collective-permute-start.1 = (f32[6,4,1,128]{3,1,2,0:T(4,128)S(1)}, f32[6,4,1,128]{3,1,2,0:T(4,128)S(1)}, u32[]{:S(2)}, u32[]{:S(2)}) collective-permute-start(f32[6,4,1,128]{3,1,2,0:T(4,128)S(1)} %bitcast.319), channel_id=1, source_target_pairs={{16,0},{32,16},{48,32},{64,48},{80,64},{96,80},{112,96},{128,112},... | collective-permute-start | bytes 36872 | tf_op jit(solution)/shard_map/ppermute | solution.py:22
  260.3 12.0 %collective-permute-start.2 = (f32[6,4,66,1]{2,1,3,0:T(4,128)S(1)}, f32[6,4,66,1]{2,1,3,0:T(4,128)S(1)}, u32[]{:S(2)}, u32[]{:S(2)}) collective-permute-start(f32[6,4,66,1]{2,1,3,0:T(4,128)S(1)} %get-tuple-element.19), channel_id=1, source_target_pairs={{0,1},{1,2},{2,3},{3,4},{4,5},{5,6},{6,7},{7,8},{8,9},{9,10},{10,1... | collective-permute-start | bytes 19016 | tf_op jit(solution)/shard_map/ppermute | solution.py:19
  263.0 9.3 %collective-permute-start.3 = (f32[6,4,66,1]{2,1,3,0:T(4,128)S(1)}, f32[6,4,66,1]{2,1,3,0:T(4,128)S(1)}, u32[]{:S(2)}, u32[]{:S(2)}) collective-permute-start(f32[6,4,66,1]{2,1,3,0:T(4,128)S(1)} %get-tuple-element.20), channel_id=1, source_target_pairs={{1,0},{2,1},{3,2},{4,3},{5,4},{6,5},{7,6},{8,7},{9,8},{10,9},{11,1... | collective-permute-start | bytes 19016 | tf_op jit(solution)/shard_map/ppermute | solution.py:22
  272.2 2.5 copy-start
  276.5 71.5 %copy-start.3 = (f32[4,66,130]{1,0,2:T(4,128)S(1)}, f32[4,66,130]{1,0,2:T(4,128)}, u32[]{:S(2)}) copy-start(f32[4,66,130]{1,0,2:T(4,128)} %get-tuple-element.14) | copy-start | bytes 411844
  276.5 71.6 %copy-start.4 = (f32[4,66,130]{1,0,2:T(4,128)S(1)}, f32[4,66,130]{1,0,2:T(4,128)}, u32[]{:S(2)}) copy-start(f32[4,66,130]{1,0,2:T(4,128)} %get-tuple-element.16) | copy-start | bytes 411844
  276.5 71.6 %copy-start.11 = (f32[3,64,128]{1,0,2:T(4,128)S(1)}, f32[3,64,128]{1,0,2:T(4,128)}, u32[]{:S(2)}) copy-start(f32[3,64,128]{1,0,2:T(4,128)} %get-tuple-element.29) | copy-start | bytes 294916
  276.5 71.6 %copy-start.12 = (f32[3,64,128]{1,0,2:T(4,128)S(1)}, f32[3,64,128]{1,0,2:T(4,128)}, u32[]{:S(2)}) copy-start(f32[3,64,128]{1,0,2:T(4,128)} %get-tuple-element.32) | copy-start | bytes 294916
  276.5 71.6 %copy-start.13 = (f32[3,64,128]{1,0,2:T(4,128)S(1)}, f32[3,64,128]{1,0,2:T(4,128)}, u32[]{:S(2)}) copy-start(f32[3,64,128]{1,0,2:T(4,128)} %get-tuple-element.33) | copy-start | bytes 294916
  276.6 71.6 %copy-start.14 = (f32[3,64,128]{1,0,2:T(4,128)S(1)}, f32[3,64,128]{1,0,2:T(4,128)}, u32[]{:S(2)}) copy-start(f32[3,64,128]{1,0,2:T(4,128)} %get-tuple-element.34) | copy-start | bytes 294916
  348.1 1.1 copy-start.1
  350.9 6.6 %copy-start.18 = (f32[3,64,128]{2,1,0:T(8,128)S(1)}, f32[3,64,128]{2,1,0:T(8,128)}, u32[]{:S(2)}) copy-start(f32[3,64,128]{2,1,0:T(8,128)} %param.6) | copy-start | bytes 294916
  350.9 7.6 %copy-start.21 = (f32[4,64,128]{2,1,0:T(8,128)S(1)}, f32[4,64,128]{2,1,0:T(8,128)}, u32[]{:S(2)}) copy-start(f32[4,64,128]{2,1,0:T(8,128)} %param.11) | copy-start | bytes 393220
  352.4 7.0 %collective-permute-start.4 = (f32[3,4,1,128]{3,1,2,0:T(4,128)S(1)}, f32[3,4,1,128]{3,1,2,0:T(4,128)S(1)}, u32[]{:S(2)}, u32[]{:S(2)}) collective-permute-start(f32[3,4,1,128]{3,1,2,0:T(4,128)S(1)} %copy.194), channel_id=1, source_target_pairs={{16,0},{32,16},{48,32},{64,48},{80,64},{96,80},{112,96},{128,112},... | collective-permute-start | bytes 18440 | tf_op jit(solution)/shard_map/ppermute | solution.py:22
  355.2 11.3 %collective-permute-start.5 = (f32[3,4,1,128]{3,1,2,0:T(4,128)}, f32[3,4,1,128]{3,1,2,0:T(4,128)}, u32[]{:S(2)}, u32[]{:S(2)}) collective-permute-start(f32[3,4,1,128]{3,1,2,0:T(4,128)} %copy.196), channel_id=1, source_target_pairs={{0,16},{16,32},{32,48},{48,64},{64,80},{80,96},{96,112},{112,128},... | collective-permute-start | bytes 18440 | tf_op jit(solution)/shard_map/ppermute | solution.py:19
  369.7 10.3 %collective-permute-start.6 = (f32[3,4,66,1]{2,1,3,0:T(4,128)}, f32[3,4,66,1]{2,1,3,0:T(4,128)S(1)}, u32[]{:S(2)}, u32[]{:S(2)}) collective-permute-start(f32[3,4,66,1]{2,1,3,0:T(4,128)} %get-tuple-element.23), channel_id=1, source_target_pairs={{1,0},{2,1},{3,2},{4,3},{5,4},{6,5},{7,6},{8,7},{9,8},{10,9},{11,1... | collective-permute-start | bytes 9512 | tf_op jit(solution)/shard_map/ppermute | solution.py:22
  375.6 8.4 %collective-permute-start.7 = (f32[3,4,66,1]{2,1,3,0:T(4,128)}, f32[3,4,66,1]{2,1,3,0:T(4,128)S(1)}, u32[]{:S(2)}, u32[]{:S(2)}) collective-permute-start(f32[3,4,66,1]{2,1,3,0:T(4,128)} %get-tuple-element.24), channel_id=1, source_target_pairs={{0,1},{1,2},{2,3},{3,4},{4,5},{5,6},{6,7},{7,8},{8,9},{9,10},{10,1... | collective-permute-start | bytes 9512 | tf_op jit(solution)/shard_map/ppermute | solution.py:19
  380.0 8.8 %copy-start.2 = (f32[3,64,128]{1,0,2:T(4,128)S(1)}, f32[3,64,128]{1,0,2:T(4,128)}, u32[]{:S(2)}) copy-start(f32[3,64,128]{1,0,2:T(4,128)} %get-tuple-element.46) | copy-start | bytes 294916
  389.3 1.1 copy-start.6
  389.3 1.1 copy-start.7
  (6 other events, 5.3 us)
Sparse Core Ops, SparseCore 0:
  11.4 105.2 all-gather.2
  244.9 99.8 all-gather.4
where the time goes:
time: 407 us; the launch traced here: 402 us
  waiting for transfers between devices  215 us (53%)
  local copies, waits for them, and re-layouts  58.5 us (14%)
  starting transfers between devices  50.5 us (12%)
  other arithmetic  24.1 us (6%)
  matrix products  19.5 us (5%)
  blocking collectives  18.9 us (5%)
  between operations  15.5 us (4%)
    all_gather x1, waiting for transfers between devices, local(): gathered = lax.all_gather(interface_velocity, 'bx', axis=1, tiled=True)  109 us
    all_gather x1, waiting for transfers between devices, local(): lax.all_gather(spatial.reshape(3, strike_length, row_block), 'bx', axis=2...  68.3 us
    ppermute x4, starting transfers between devices, extended(): lax.ppermute(lax.slice_in_dim(block, 0, width, axis=dim), axis, backward)  23.4 us
    all_to_all x1, blocking collectives, strike_modes(): return lax.all_to_all(block, 'bx', split_axis=4, concat_axis=4, tiled=True)  18.9 us
    unnamed x66, local copies, waits for them, and re-layouts  14.5 us
    all_to_all x1, waiting for transfers between devices, strike_modes(): return lax.all_to_all(block, 'bx', split_axis=4, concat_axis=4, tiled=True)  14.2 us
    all_to_all x2, waiting for transfers between devices, dip_blocks(): return lax.all_to_all(block, 'by', split_axis=2, concat_axis=2, tiled=True)  12.4 us
    all_to_all x2, starting transfers between devices, dip_blocks(): return lax.all_to_all(block, 'by', split_axis=2, concat_axis=2, tiled=True)  11.6 us
  transfers between devices with their start and end apart: 13, of which 7 were waited for; matrix products, arithmetic and copies ran while one was open for 5% of the time, Pallas kernels for 0%

commit v1 on v0

--- a/solution.py
+++ b/solution.py
@@ -8,6 +8,13 @@
 COURANT = 0.3
 FRICTION = 0.6
 HIGHEST = lax.Precision.HIGHEST
+
+
+def stacked_exchange(shard, axis, split, join):
+    peers = lax.axis_size(axis)
+    blocks = jnp.stack(jnp.split(shard, peers, axis=split), axis=0)
+    blocks = lax.all_to_all(blocks, axis, split_axis=0, concat_axis=0)
+    return jnp.concatenate(blocks, axis=join)
 
 
 def extended(block, sides, width):
@@ -58,7 +65,7 @@
 
 
 def strike_modes(block):
-    return lax.all_to_all(block, "bx", split_axis=4, concat_axis=4, tiled=True)
+    return stacked_exchange(block, "bx", 4, 4)
 
 
 def widen(fields):

time: 407 us -> 441 us (1.084)
  other arithmetic: 24.1 us -> 49.6 us
  local copies, waits for them, and re-layouts: 58.5 us -> 63.2 us
    unnamed x5 -> x67, other arithmetic: 0.93 us -> 26.3 us
    another operation x2 -> x1, local copies, waits for them, and re-layouts: 1.75 us -> 6.47 us  [stacked_exchange(): blocks = jnp.stack(jnp.split(shard, peers, axis=split), axis=0)]
    unnamed x66 -> x60, local copies, waits for them, and re-layouts: 14.5 us -> 13.8 us
  transfers between devices with their start and end apart: 13 -> 13, of which waited for: 7 -> 7; matrix products, arithmetic and copies ran while one was open for 5% -> 4% of each run, Pallas kernels for 0% -> 0%
where the time goes in v1:
time: 441 us; the launch traced here: 436 us
  waiting for transfers between devices  216 us (49%)
  local copies, waits for them, and re-layouts  63.2 us (14%)
  starting transfers between devices  50.1 us (11%)
  other arithmetic  49.6 us (11%)
  matrix products  23 us (5%)
  blocking collectives  19.1 us (4%)
  between operations  15.3 us (3%)
    all_gather x1, waiting for transfers between devices, local(): gathered = lax.all_gather(interface_velocity, 'bx', axis=1, tiled=True)  109 us
    all_gather x1, waiting for transfers between devices, local(): lax.all_gather(spatial.reshape(3, strike_length, row_block), 'bx', axis=2...  68.3 us
    unnamed x67, other arithmetic  26.3 us
    ppermute x4, starting transfers between devices, extended(): lax.ppermute(lax.slice_in_dim(block, 0, width, axis=dim), axis, backward)  23.4 us
    all_to_all x1, blocking collectives, stacked_exchange(): blocks = lax.all_to_all(blocks, axis, split_axis=0, concat_axis=0)  19.1 us
    all_to_all x1, waiting for transfers between devices, stacked_exchange(): blocks = lax.all_to_all(blocks, axis, split_axis=0, concat_axis=0)  14.8 us
    unnamed x60, local copies, waits for them, and re-layouts  13.8 us
    all_to_all x2, waiting for transfers between devices, dip_blocks(): return lax.all_to_all(block, 'by', split_axis=2, concat_axis=2, tiled=True)  12.4 us
  transfers between devices with their start and end apart: 13, of which 7 were waited for; matrix products, arithmetic and copies ran while one was open for 4% of the time, Pallas kernels for 0%

profile of v1, /device:TPU:6, one launch (start us, length us, event | category | flops | bytes accessed | tf_op | source)
XLA Modules:
  0.0 436.0 jit_solution(15239852054889276096)
XLA Ops:
  8.0 108.7 %all-gather.3.cloned.1.call-done = f32[3,2048,128]{2,1,0:T(8,128)} async-done(((f32[3,64,128]{2,1,0:T(8,128)}), f32[3,2048,128]{2,1,0:T(8,128)}) %all-gather.3.cloned.1.call-update) | async-done | bytes 3145744 | tf_op jit(solution)/shard_map/all_gather | solution.py:159
  116.7 2.8 constant_dynamic-slice_fusion
  124.5 5.5 %all-to-all-start = ((f32[2,3,64,128]{3,0,1,2:T(2,128)}), f32[2,3,64,128]{3,0,1,2:T(2,128)S(1)}, u32[]{:S(2)}, u32[]{:S(2)}) async-start(f32[2,3,64,128]{3,0,1,2:T(2,128)} %copy.394), calls=%async_computation | async-start | bytes 393216 | tf_op jit(solution)/shard_map/all_to_all | solution.py:64
  131.5 6.1 %all-to-all-done = f32[2,3,64,128]{3,0,1,2:T(2,128)S(1)} async-done(((f32[2,3,64,128]{3,0,1,2:T(2,128)}), f32[2,3,64,128]{3,0,1,2:T(2,128)S(1)}, u32[]{:S(2)}, u32[]{:S(2)}) %all-to-all-start) | async-done | bytes 196640 | tf_op jit(solution)/shard_map/all_to_all | solution.py:64
  138.7 3.4 reshape.264
  146.2 4.2 reshape.265
  156.8 1.9 reshape.268
  158.7 6.0 %all-to-all-start.1 = ((f32[32,1,1536]{2,1,0:T(1,128)}), f32[32,1,1536]{2,1,0:T(1,128)S(1)}, u32[]{:S(2)}, u32[]{:S(2)}) async-start(f32[32,1,1536]{2,1,0:T(1,128)} %reshape.268), calls=%async_computation.1 | async-start | bytes 393216 | tf_op jit(solution)/shard_map/all_to_all | solution.py:16
  165.6 14.8 %all-to-all-done.1 = f32[32,1,1536]{2,1,0:T(1,128)S(1)} async-done(((f32[32,1,1536]{2,1,0:T(1,128)}), f32[32,1,1536]{2,1,0:T(1,128)S(1)}, u32[]{:S(2)}, u32[]{:S(2)}) %all-to-all-start.1) | async-done | bytes 196640 | tf_op jit(solution)/shard_map/all_to_all | solution.py:16
  217.2 6.5 %copy.409 = f32[32,2,3,16,4,4]{3,5,4,2,1,0:T(4,128)S(1)} copy(f32[32,2,3,16,4,4]{5,3,4,2,1,0:T(8,128)} %fusion.132) | data formatting | bytes 393216 | tf_op jit(solution)/shard_map/stack | solution.py:15
  224.9 19.1 %all_to_all.20 = f32[32,1,1536]{2,1,0:T(1,128)S(1)} all-to-all(f32[32,1,1536]{2,1,0:T(1,128)S(1)} %reshape.270), channel_id=1, replica_groups=mesh['bx'=32,'by'=16] {'bx'}, dimensions={0} | all-to-all | bytes 393216 | tf_op jit(solution)/shard_map/all_to_all | solution.py:16
  251.0 2.2 copy.413
  253.2 3.2 stack.352
  259.3 2.6 stack.353
  262.8 5.8 %all-to-all-start.3 = ((f32[2,3,64,128]{3,0,1,2:T(2,128)}), f32[2,3,64,128]{3,0,1,2:T(2,128)S(1)}, u32[]{:S(2)}, u32[]{:S(2)}) async-start(f32[2,3,64,128]{3,0,1,2:T(2,128)} %copy.417), calls=%async_computation.3 | async-start | bytes 393216 | tf_op jit(solution)/shard_map/all_to_all | solution.py:64
  268.8 6.4 %all-to-all-done.3 = f32[2,3,64,128]{3,0,1,2:T(2,128)S(1)} async-done(((f32[2,3,64,128]{3,0,1,2:T(2,128)}), f32[2,3,64,128]{3,0,1,2:T(2,128)S(1)}, u32[]{:S(2)}, u32[]{:S(2)}) %all-to-all-start.3) | async-done | bytes 196640 | tf_op jit(solution)/shard_map/all_to_all | solution.py:64
  279.2 1.9 collective-permute-start
  281.1 9.7 %collective-permute-start.1 = (f32[6,4,1,128]{3,1,2,0:T(4,128)S(1)}, f32[6,4,1,128]{3,1,2,0:T(4,128)S(1)}, u32[]{:S(2)}, u32[]{:S(2)}) collective-permute-start(f32[6,4,1,128]{3,1,2,0:T(4,128)S(1)} %bitcast.577), channel_id=1, source_target_pairs={{16,0},{32,16},{48,32},{64,48},{80,64},{96,80},{112,96},{128,112},... | collective-permute-start | bytes 36872 | tf_op jit(solution)/shard_map/ppermute | solution.py:29
  294.7 2.7 collective-permute-start.2
  297.3 5.9 %collective-permute-start.3 = (f32[6,4,66,1]{2,1,3,0:T(4,128)S(1)}, f32[6,4,66,1]{2,1,3,0:T(4,128)S(1)}, u32[]{:S(2)}, u32[]{:S(2)}) collective-permute-start(f32[6,4,66,1]{2,1,3,0:T(4,128)S(1)} %get-tuple-element.22), channel_id=1, source_target_pairs={{1,0},{2,1},{3,2},{4,3},{5,4},{6,5},{7,6},{8,7},{9,8},{10,9},{11,1... | collective-permute-start | bytes 19016 | tf_op jit(solution)/shard_map/ppermute | solution.py:29
  304.5 2.1 copy.430
  306.6 2.5 maximum_bitcast_fusion.2
  310.9 68.3 %all-gather.5.cloned.1.call-done = f32[3,2048,128]{1,0,2:T(4,128)} async-done(((f32[3,2048,4]{1,0,2:T(4,128)}), f32[3,2048,128]{1,0,2:T(4,128)}) %all-gather.5.cloned.1.call-update) | async-done | bytes 3145744 | tf_op jit(solution)/shard_map/all_gather | solution.py:218
  380.5 1.9 fusion.27
  386.7 1.9 collective-permute-start.4
  389.5 2.4 collective-permute-start.5
  394.0 6.7 %collective-permute-done.5 = f32[3,4,1,128]{3,1,2,0:T(4,128)} collective-permute-done((f32[3,4,1,128]{3,1,2,0:T(4,128)}, f32[3,4,1,128]{3,1,2,0:T(4,128)}, u32[]{:S(2)}, u32[]{:S(2)}) %collective-permute-start.5) | collective-permute-done | bytes 6176 | tf_op jit(solution)/shard_map/ppermute | solution.py:26
  400.7 1.9 copy.434
  404.0 5.9 %collective-permute-start.6 = (f32[3,4,66,1]{2,1,3,0:T(4,128)}, f32[3,4,66,1]{2,1,3,0:T(4,128)S(1)}, u32[]{:S(2)}, u32[]{:S(2)}) collective-permute-start(f32[3,4,66,1]{2,1,3,0:T(4,128)} %get-tuple-element.25), channel_id=1, source_target_pairs={{1,0},{2,1},{3,2},{4,3},{5,4},{6,5},{7,6},{8,7},{9,8},{10,9},{11,1... | collective-permute-start | bytes 9512 | tf_op jit(solution)/shard_map/ppermute | solution.py:29
  409.9 2.1 collective-permute-start.7
  414.2 4.1 collective-permute-done.7
  418.4 4.8 %fusion.11 = (f32[3,4,64,128]{2,1,3,0:T(4,128)S(1)}, f32[3,4,64,128]{2,1,3,0:T(4,128)S(1)}) fusion(f32[3,4,66,1]{2,1,3,0:T(4,128)S(1)} %collective-permute-done.7, f32[3,4,1,128]{2,1,3,0:T(4,128)S(1)} %copy.432, f32[3,4,64,128]{2,1,3,0:T(4,128)S(1)} %fusion.14, f32[3,4,1,128]{2,1,3,0:T(4,128)} %copy.434, f32[3,4,66,1]{2,1,3,0:T(4,128)S(1)} %collective-permute-done.6), kind=kLoop, calls=%fused_computation.155 | loop fusion | flops 1179648 | bytes 1198272 | tf_op jit(solution)/shard_map/mul | solution.py:80
  (226 shorter events, 96.9 us)
Async XLA Ops:
  7.2 109.5 %all-gather.3.cloned.1.call-start = ((), (), s32[]{:S(2)}) async-start(), calls=%async_computation.4 | async-start | bytes 3244032 | tf_op jit(solution)/shard_map/all_gather | solution.py:159
  123.1 7.7 %copy-start.20 = (f32[7,4,1,16,128]{4,3,2,1,0:T(8,128)S(1)}, f32[7,4,1,16,128]{4,3,2,1,0:T(8,128)}, u32[]{:S(2)}) copy-start(f32[7,4,1,16,128]{4,3,2,1,0:T(8,128)} %param.8) | copy-start | bytes 688132
  124.5 13.0 %all-to-all-start = ((f32[2,3,64,128]{3,0,1,2:T(2,128)}), f32[2,3,64,128]{3,0,1,2:T(2,128)S(1)}, u32[]{:S(2)}, u32[]{:S(2)}) async-start(f32[2,3,64,128]{3,0,1,2:T(2,128)} %copy.394), calls=%async_computation | async-start | bytes 393216 | tf_op jit(solution)/shard_map/all_to_all | solution.py:64
  156.8 7.9 %copy-start.16 = (f32[4,16,128,6]{2,1,0,3:T(8,128)S(1)}, f32[4,16,128,6]{2,1,0,3:T(8,128)}, u32[]{:S(2)}) copy-start(f32[4,16,128,6]{2,1,0,3:T(8,128)} %slice_bitcast_fusion.16) | copy-start | bytes 589828
  156.8 7.9 %copy-start.5 = (f32[6,2,3,4,1,16,128]{6,5,4,3,2,1,0:T(8,128)S(1)}, f32[6,2,3,4,1,16,128]{6,5,4,3,2,1,0:T(8,128)}, u32[]{:S(2)}) copy-start(f32[6,2,3,4,1,16,128]{6,5,4,3,2,1,0:T(8,128)} %param.7) | copy-start | bytes 3538948
  158.7 21.7 %all-to-all-start.1 = ((f32[32,1,1536]{2,1,0:T(1,128)}), f32[32,1,1536]{2,1,0:T(1,128)S(1)}, u32[]{:S(2)}, u32[]{:S(2)}) async-start(f32[32,1,1536]{2,1,0:T(1,128)} %reshape.268), calls=%async_computation.1 | async-start | bytes 393216 | tf_op jit(solution)/shard_map/all_to_all | solution.py:16
  259.3 2.6 copy-start.17
  262.8 12.4 %all-to-all-start.3 = ((f32[2,3,64,128]{3,0,1,2:T(2,128)}), f32[2,3,64,128]{3,0,1,2:T(2,128)S(1)}, u32[]{:S(2)}, u32[]{:S(2)}) async-start(f32[2,3,64,128]{3,0,1,2:T(2,128)} %copy.417), calls=%async_computation.3 | async-start | bytes 393216 | tf_op jit(solution)/shard_map/all_to_all | solution.py:64
  268.5 110.7 %all-gather.5.cloned.1.call-start = ((), (), s32[]{:S(2)}) async-start(), calls=%async_computation.5 | async-start | bytes 4325376 | tf_op jit(solution)/shard_map/all_gather | solution.py:218
  276.6 2.6 copy-start.15
  279.2 12.3 %collective-permute-start = (f32[6,4,1,128]{3,1,2,0:T(4,128)S(1)}, f32[6,4,1,128]{3,1,2,0:T(4,128)S(1)}, u32[]{:S(2)}, u32[]{:S(2)}) collective-permute-start(f32[6,4,1,128]{3,1,2,0:T(4,128)S(1)} %bitcast.578), channel_id=1, source_target_pairs={{0,16},{16,32},{32,48},{48,64},{64,80},{80,96},{96,112},{112,128},... | collective-permute-start | bytes 36872 | tf_op jit(solution)/shard_map/ppermute | solution.py:26
  281.1 11.2 %collective-permute-start.1 = (f32[6,4,1,128]{3,1,2,0:T(4,128)S(1)}, f32[6,4,1,128]{3,1,2,0:T(4,128)S(1)}, u32[]{:S(2)}, u32[]{:S(2)}) collective-permute-start(f32[6,4,1,128]{3,1,2,0:T(4,128)S(1)} %bitcast.577), channel_id=1, source_target_pairs={{16,0},{32,16},{48,32},{64,48},{80,64},{96,80},{112,96},{128,112},... | collective-permute-start | bytes 36872 | tf_op jit(solution)/shard_map/ppermute | solution.py:29
  294.7 12.0 %collective-permute-start.2 = (f32[6,4,66,1]{2,1,3,0:T(4,128)S(1)}, f32[6,4,66,1]{2,1,3,0:T(4,128)S(1)}, u32[]{:S(2)}, u32[]{:S(2)}) collective-permute-start(f32[6,4,66,1]{2,1,3,0:T(4,128)S(1)} %get-tuple-element.21), channel_id=1, source_target_pairs={{0,1},{1,2},{2,3},{3,4},{4,5},{5,6},{6,7},{7,8},{8,9},{9,10},{10,1... | collective-permute-start | bytes 19016 | tf_op jit(solution)/shard_map/ppermute | solution.py:26
  297.3 9.3 %collective-permute-start.3 = (f32[6,4,66,1]{2,1,3,0:T(4,128)S(1)}, f32[6,4,66,1]{2,1,3,0:T(4,128)S(1)}, u32[]{:S(2)}, u32[]{:S(2)}) collective-permute-start(f32[6,4,66,1]{2,1,3,0:T(4,128)S(1)} %get-tuple-element.22), channel_id=1, source_target_pairs={{1,0},{2,1},{3,2},{4,3},{5,4},{6,5},{7,6},{8,7},{9,8},{10,9},{11,1... | collective-permute-start | bytes 19016 | tf_op jit(solution)/shard_map/ppermute | solution.py:29
  306.6 2.5 copy-start
  310.9 71.5 %copy-start.3 = (f32[4,66,130]{1,0,2:T(4,128)S(1)}, f32[4,66,130]{1,0,2:T(4,128)}, u32[]{:S(2)}) copy-start(f32[4,66,130]{1,0,2:T(4,128)} %get-tuple-element.16) | copy-start | bytes 411844
  310.9 71.5 %copy-start.4 = (f32[4,66,130]{1,0,2:T(4,128)S(1)}, f32[4,66,130]{1,0,2:T(4,128)}, u32[]{:S(2)}) copy-start(f32[4,66,130]{1,0,2:T(4,128)} %get-tuple-element.18) | copy-start | bytes 411844
  310.9 71.5 %copy-start.11 = (f32[3,64,128]{1,0,2:T(4,128)S(1)}, f32[3,64,128]{1,0,2:T(4,128)}, u32[]{:S(2)}) copy-start(f32[3,64,128]{1,0,2:T(4,128)} %get-tuple-element.31) | copy-start | bytes 294916
  310.9 71.5 %copy-start.12 = (f32[3,64,128]{1,0,2:T(4,128)S(1)}, f32[3,64,128]{1,0,2:T(4,128)}, u32[]{:S(2)}) copy-start(f32[3,64,128]{1,0,2:T(4,128)} %get-tuple-element.34) | copy-start | bytes 294916
  310.9 71.5 %copy-start.13 = (f32[3,64,128]{1,0,2:T(4,128)S(1)}, f32[3,64,128]{1,0,2:T(4,128)}, u32[]{:S(2)}) copy-start(f32[3,64,128]{1,0,2:T(4,128)} %get-tuple-element.35) | copy-start | bytes 294916
  310.9 71.5 %copy-start.14 = (f32[3,64,128]{1,0,2:T(4,128)S(1)}, f32[3,64,128]{1,0,2:T(4,128)}, u32[]{:S(2)}) copy-start(f32[3,64,128]{1,0,2:T(4,128)} %get-tuple-element.36) | copy-start | bytes 294916
  382.4 1.1 copy-start.1
  385.3 6.6 %copy-start.18 = (f32[3,64,128]{2,1,0:T(8,128)S(1)}, f32[3,64,128]{2,1,0:T(8,128)}, u32[]{:S(2)}) copy-start(f32[3,64,128]{2,1,0:T(8,128)} %param.6) | copy-start | bytes 294916
  385.3 7.6 %copy-start.21 = (f32[4,64,128]{2,1,0:T(8,128)S(1)}, f32[4,64,128]{2,1,0:T(8,128)}, u32[]{:S(2)}) copy-start(f32[4,64,128]{2,1,0:T(8,128)} %param.11) | copy-start | bytes 393220
  386.7 7.0 %collective-permute-start.4 = (f32[3,4,1,128]{3,1,2,0:T(4,128)S(1)}, f32[3,4,1,128]{3,1,2,0:T(4,128)S(1)}, u32[]{:S(2)}, u32[]{:S(2)}) collective-permute-start(f32[3,4,1,128]{3,1,2,0:T(4,128)S(1)} %copy.431), channel_id=1, source_target_pairs={{16,0},{32,16},{48,32},{64,48},{80,64},{96,80},{112,96},{128,112},... | collective-permute-start | bytes 18440 | tf_op jit(solution)/shard_map/ppermute | solution.py:29
  389.5 11.3 %collective-permute-start.5 = (f32[3,4,1,128]{3,1,2,0:T(4,128)}, f32[3,4,1,128]{3,1,2,0:T(4,128)}, u32[]{:S(2)}, u32[]{:S(2)}) collective-permute-start(f32[3,4,1,128]{3,1,2,0:T(4,128)} %copy.433), channel_id=1, source_target_pairs={{0,16},{16,32},{32,48},{48,64},{64,80},{80,96},{96,112},{112,128},... | collective-permute-start | bytes 18440 | tf_op jit(solution)/shard_map/ppermute | solution.py:26
  404.0 10.2 %collective-permute-start.6 = (f32[3,4,66,1]{2,1,3,0:T(4,128)}, f32[3,4,66,1]{2,1,3,0:T(4,128)S(1)}, u32[]{:S(2)}, u32[]{:S(2)}) collective-permute-start(f32[3,4,66,1]{2,1,3,0:T(4,128)} %get-tuple-element.25), channel_id=1, source_target_pairs={{1,0},{2,1},{3,2},{4,3},{5,4},{6,5},{7,6},{8,7},{9,8},{10,9},{11,1... | collective-permute-start | bytes 9512 | tf_op jit(solution)/shard_map/ppermute | solution.py:29
  409.9 8.4 %collective-permute-start.7 = (f32[3,4,66,1]{2,1,3,0:T(4,128)}, f32[3,4,66,1]{2,1,3,0:T(4,128)S(1)}, u32[]{:S(2)}, u32[]{:S(2)}) collective-permute-start(f32[3,4,66,1]{2,1,3,0:T(4,128)} %get-tuple-element.26), channel_id=1, source_target_pairs={{0,1},{1,2},{2,3},{3,4},{4,5},{5,6},{6,7},{7,8},{8,9},{9,10},{10,1... | collective-permute-start | bytes 9512 | tf_op jit(solution)/shard_map/ppermute | solution.py:26
  414.2 8.9 %copy-start.2 = (f32[3,64,128]{1,0,2:T(4,128)S(1)}, f32[3,64,128]{1,0,2:T(4,128)}, u32[]{:S(2)}) copy-start(f32[3,64,128]{1,0,2:T(4,128)} %get-tuple-element.46) | copy-start | bytes 294916
  423.4 1.0 copy-start.9
  423.6 1.1 copy-start.6
  423.6 1.1 copy-start.7
  (5 other events, 4.3 us)
Sparse Core Ops, SparseCore 0:
  11.4 105.2 all-gather.2
  279.3 99.8 all-gather.4
